TPU v7x, 128 devices: a whole 4x4x4 slice. The times are simulated.
128 devices in a mesh: horiz: 8 (over x, y_lo), vert: 16 (over z, y_hi, core).
Axes of the slice: x: 4, y: 4 (y_hi: 2, y_lo: 2; y = y_hi * 2 + y_lo), z: 4, core: 2. Of those that a mesh axis runs over, the one named last changes fastest.
Arguments:
- air_seed: float32 [5, 256, 256, 256], P(None, 'vert', 'horiz'), may hold values from -6 to 6
- wall_seed: float32 [8, 131072], P(None, ('horiz', 'vert')), may hold values from -6 to 6
- speed: float32 [3, 256, 256, 256], P(None, 'vert', 'horiz'), may hold values from 0.01 to 0.08
- upwind: int32 [3, 256, 256, 256], P(None, 'vert', 'horiz'), may hold values 0 or 1
- diffusivity: float32 [5], replicated, may hold values from 0.01 to 0.06
- conductivity: float32 [7, 131072], P(None, ('horiz', 'vert')), may hold values from 0.02 to 0.2
- wall_saved: float32 [4, 8, 131072], P(None, None, ('horiz', 'vert')), may hold values from -6 to 6
- heat_table: float32 [8], replicated, may hold values from 0.05 to 0.4
- interface: int32 [131072], P(('horiz', 'vert')), may hold values from 0 to 131071
- owner: int32 [131072, 1], P(('horiz', 'vert')), may hold values from 0 to 15; in each aligned block of 1024 rows (0 to 1023, 1024 to 2047, ...) at most 256 rows name the same one
- material: int32 [131072], P(('horiz', 'vert')), may hold values from 0 to 7
Outputs:
- air_adjoint: float32 [5, 256, 256, 256], P(None, 'vert', 'horiz')
- wall_adjoint: float32 [8, 131072], P(None, ('horiz', 'vert'))
- conductivity_grad: float32 [7, 131072], P(None, ('horiz', 'vert'))
Inputs may be any that keep to these rules, and one draw needn't show every extreme that they name: `owner`: in each aligned block of 1024 wall columns (those of one device) at most 256 columns name one vertical brick, and in every draw some brick is named by exactly 256 of them.
All inputs are finite; a program needn't handle non-finite values. No bound on the sum of `upwind` on one device may be relied on, other than what follows from the above.
Results may differ from a plain program's by a relative error of at most 0.00014.
Values sent between devices are 32-bit elements; how exact they have to be, the bound alone decides.
A program may use at most 128 MiB of HBM per device.

v0:
```python
import functools

import jax
import jax.numpy as jnp
from jax import lax
from jax.experimental import pallas as pl
from jax.experimental.pallas import tpu as pltpu
from jax.sharding import PartitionSpec as P

F32, BF16, I32 = jnp.float32, jnp.bfloat16, jnp.int32
MESH = pl.DeviceIdType.MESH
LANES, SUBS = 128, 8
RATIO = 0.5
ROWS = 8
NT = (((1,), (1,)), ((), ()))


def dot(a, b):
    return jnp.dot(a, b, preferred_element_type=F32)


def dot_nt(a, b):
    return lax.dot_general(a, b, NT, preferred_element_type=F32)


def split(value, parts):
    pieces = []
    for _ in range(parts):
        piece = value.astype(BF16).astype(F32)
        pieces.append(piece)
        value = value - piece
    return pieces


def wall_back(p, cond8):
    flux = cond8 * (pltpu.roll(p, ROWS - 1, 0) - p)
    return p + flux - pltpu.roll(flux, 1, 0)


def kernel(
    dims,
    kappa_ref,
    table_ref,
    wall_ref,
    cond_ref,
    saved_ref,
    face_ref,
    owner_ref,
    mat_ref,
    air_hbm,
    speed_hbm,
    upwind_hbm,
    air_out,
    wall_out,
    grad_out,
    air,
    speed,
    upwind,
    in_z,
    in_x,
    in_y,
    centre_c,
    out_x_last,
    in_x_last,
    in_z_halo,
    in_x_halo,
    halo_z,
    halo_x,
    edge_x,
    fix_x,
    field_hi,
    field_lo,
    row_hot,
    col_hot,
    added,
    parts_ref,
    rank_hot,
    parcel,
    served,
    result,
    returned,
    load_sem,
    store_sem,
    in_send,
    in_recv,
    halo_send,
    halo_recv,
    parcel_send,
    parcel_recv,
    return_send,
    return_recv,
):
    steps, groups, columns = dims
    fields, depth, breadth, span = air_out.shape
    walls = face_ref.shape[1]
    cap = rank_hot.shape[0]
    rows = depth * breadth
    x_tiles = breadth // SUBS
    me = lax.axis_index("vert")
    col = lax.axis_index("horiz")
    above, below = lax.rem(me + 1, groups), lax.rem(me + groups - 1, groups)
    east, west = lax.rem(col + 1, columns), lax.rem(col + columns - 1, columns)
    has_below = jnp.where(me > 0, 1.0, 0.0).astype(F32)
    has_above = jnp.where(me < groups - 1, 1.0, 0.0).astype(F32)
    has_west = jnp.where(col > 0, 1.0, 0.0).astype(F32)
    has_east = jnp.where(col < columns - 1, 1.0, 0.0).astype(F32)

    loads = [
        pltpu.make_async_copy(air_hbm, air.at[0, :, pl.ds(1, depth)], load_sem.at[0]),
        pltpu.make_async_copy(speed_hbm, speed, load_sem.at[1]),
        pltpu.make_async_copy(upwind_hbm, upwind, load_sem.at[2]),
    ]
    for load in loads:
        load.start()

    barrier = pltpu.get_barrier_semaphore()

    def greet(d, carry):
        pl.semaphore_signal(
            barrier, inc=1, device_id={"vert": lax.rem(me + d, groups)}, device_id_type=MESH
        )
        return carry

    lax.fori_loop(1, groups, greet, 0)
    for neighbour in (east, west):
        pl.semaphore_signal(barrier, inc=1, device_id={"horiz": neighbour}, device_id_type=MESH)

    plane0 = jnp.zeros((fields, breadth, span), F32)
    for slot in range(2):
        air[slot, :, 0] = plane0
        air[slot, :, depth + 1] = plane0
    in_z[0] = jnp.zeros((breadth, span), F32)

    material = mat_ref[...]
    hcoef = jnp.zeros(material.shape, F32)
    for k in range(table_ref.shape[0]):
        hcoef = jnp.where(material == k, table_ref[k], hcoef)
    layer = lax.broadcasted_iota(I32, (ROWS, walls), 0)
    surface = (layer == 0).astype(F32)
    cond8 = jnp.concatenate([cond_ref[...], jnp.zeros((1, walls), F32)], axis=0)
    h_top = surface * hcoef
    p = wall_ref[...]
    e = surface
    values = [face_ref[...].astype(F32), hcoef]
    for step in range(steps):
        values.append(p[0:1])
        if step < steps - 1:
            p = wall_back(p, cond8) - h_top * p
    for _ in range(steps - 2):
        e = wall_back(e, cond8) - h_top * e
        values.append(e[0:1])
    values = jnp.concatenate(values, axis=0)

    owners = owner_ref[...]
    owned = (lax.broadcasted_iota(I32, (groups, walls), 0) == owners).astype(F32)
    block = 2 * LANES
    blocks = walls // block
    stacked = jnp.concatenate(
        [owned[:, k * block : (k + 1) * block] for k in range(blocks)], axis=0
    )
    lower = (
        lax.broadcasted_iota(I32, (block, block), 0) < lax.broadcasted_iota(I32, (block, block), 1)
    ).astype(F32)
    before = dot(stacked.astype(BF16), lower.astype(BF16))
    totals = jnp.sum(stacked, axis=1, keepdims=True)
    offset = jnp.zeros((groups, 1), F32)
    ranks = []
    for k in range(blocks):
        part = slice(k * groups, (k + 1) * groups)
        ranks.append(
            jnp.sum(stacked[part] * (before[part] + offset), axis=0, keepdims=True)
        )
        offset = offset + totals[part]
    ranks = jnp.concatenate(ranks, axis=1).astype(I32)
    rank_hot[...] = (
        (lax.broadcasted_iota(I32, (cap, walls), 0) == ranks).astype(F32).astype(BF16)
    )
    for s, piece in enumerate(split(values, 3)):
        for b in range(0, groups, 2):
            pair = jnp.concatenate([piece * owned[b : b + 1], piece * owned[b + 1 : b + 2]], axis=0)
            parts_ref[pl.ds((s * groups + b) * ROWS, 2 * ROWS), :] = pair.astype(BF16)
    placed = dot_nt(parts_ref[...], rank_hot[...])
    n = groups * ROWS
    parcel[...] = placed[:n] + placed[n : 2 * n] + placed[2 * n :]
    served[pl.ds(pl.multiple_of(me * ROWS, ROWS), ROWS), :] = parcel[
        pl.ds(pl.multiple_of(me * ROWS, ROWS), ROWS), :
    ]
    result[...] = jnp.zeros_like(result)

    pl.semaphore_wait(barrier, groups + 1)

    def parcel_copy(d, src, dst, send, recv):
        to = lax.rem(me + d, groups)
        return pltpu.make_async_remote_copy(
            src_ref=src.at[pl.ds(pl.multiple_of(to * ROWS, ROWS), ROWS)],
            dst_ref=dst.at[pl.ds(pl.multiple_of(me * ROWS, ROWS), ROWS)],
            send_sem=send.at[d],
            recv_sem=recv.at[d],
            device_id={"vert": to},
            device_id_type=MESH,
        )

    def send_parcel(d, carry):
        parcel_copy(d, parcel, served, parcel_send, parcel_recv).start()
        return carry

    lax.fori_loop(1, groups, send_parcel, 0)

    def halo_copies(step, slot):
        return [
            pltpu.make_async_remote_copy(
                src_ref=src,
                dst_ref=dst,
                send_sem=halo_send.at[step, k],
                recv_sem=halo_recv.at[step, k],
                device_id=to,
                device_id_type=MESH,
            )
            for k, (src, dst, to) in enumerate(
                [
                    (air.at[slot, :, depth], halo_z.at[step, 0], {"vert": above}),
                    (air.at[slot, :, 1], halo_z.at[step, 1], {"vert": below}),
                    (edge_x.at[step, 1], halo_x.at[step, 0], {"horiz": east}),
                    (edge_x.at[step, 0], halo_x.at[step, 1], {"horiz": west}),
                ]
            )
        ]

    def split_plane(slot, z):
        plane = air[slot, 0, z + 1]
        hi = plane.astype(BF16)
        at = pl.ds(pl.multiple_of(z * breadth, breadth), breadth)
        field_hi[at, :] = hi
        field_lo[at, :] = (plane - hi.astype(F32)).astype(BF16)

    loads[0].wait()

    def pack_first(z, carry):
        for f in range(fields):
            edge_x[0, 0, f, pl.ds(z, 1), :] = air[0, f, z + 1, 0:1, :]
            edge_x[0, 1, f, pl.ds(z, 1), :] = air[0, f, z + 1, breadth - 1 : breadth, :]
        split_plane(0, z)
        return carry

    lax.fori_loop(0, depth, pack_first, 0)
    for copy in halo_copies(0, 0):
        copy.start()

    loads[1].wait()
    loads[2].wait()
    row_id = lax.broadcasted_iota(I32, (breadth, span), 0)
    lane_id = lax.broadcasted_iota(I32, (breadth, span), 1)

    def coefficients(z, carry):
        out, inn = [], []
        for d in range(3):
            s = speed[d, z]
            o = s * upwind[d, z].astype(F32)
            out.append(o)
            inn.append(s - o)
            speed[d, z] = o
        in_z[z + 1] = -inn[0]
        in_x_last[pl.ds(z, 1), :] = -inn[1][breadth - 1 : breadth]
        out_x_last[pl.ds(z, 1), :] = out[1][breadth - 1 : breadth]
        low_x = jnp.where(row_id == 0, 0.0, pltpu.roll(-inn[1], 1, 0))
        low_y = jnp.where(lane_id == 0, 0.0, pltpu.roll(-inn[2], 1, 1))
        in_x[z] = low_x
        in_y[z] = low_y
        centre_c[z] = 1.0 - (out[0] + out[1] + out[2]) - (in_z[z] + low_x + low_y)
        return carry

    lax.fori_loop(0, depth, coefficients, 0)
    in_copies = [
        pltpu.make_async_remote_copy(
            src_ref=src,
            dst_ref=dst,
            send_sem=in_send.at[k],
            recv_sem=in_recv.at[k],
            device_id=to,
            device_id_type=MESH,
        )
        for k, (src, dst, to) in enumerate(
            [
                (in_z.at[depth], in_z_halo, {"vert": above}),
                (in_x_last, in_x_halo, {"horiz": east}),
            ]
        )
    ]
    for copy in in_copies:
        copy.start()

    def wait_parcel(d, carry):
        parcel_copy(d, parcel, served, parcel_send, parcel_recv).wait()
        return carry

    lax.fori_loop(1, groups, wait_parcel, 0)

    def one_hots(s, carry):
        cell = served[pl.ds(pl.multiple_of(s * ROWS, ROWS), ROWS), :][0:1].astype(I32)
        row_hot[s] = (
            (lax.broadcasted_iota(I32, (rows, cap), 0) == cell // span).astype(F32).astype(BF16)
        )
        col_hot[s] = (
            (lax.broadcasted_iota(I32, (span, cap), 0) == cell % span).astype(F32).astype(BF16)
        )
        return carry

    lax.fori_loop(0, groups, one_hots, 0)

    sub8 = lax.broadcasted_iota(I32, (SUBS, LANES), 0)
    lane8 = lax.broadcasted_iota(I32, (SUBS, LANES), 1)

    def stencil(cur, new, z):
        zero = jnp.zeros((SUBS, LANES), F32)
        first_lane, last_lane = lane8 == 0, lane8 == LANES - 1
        first_sub, last_sub = sub8 == 0, sub8 == SUBS - 1
        for f in range(fields):
            kappa = kappa_ref[f]
            tile = {}
            for i in range(x_tiles):
                for h in range(2):
                    tile[i, h] = air[
                        cur, f, z + 1, SUBS * i : SUBS * (i + 1), LANES * h : LANES * (h + 1)
                    ]
            down = {k: pltpu.roll(t, 1, 0) for k, t in tile.items()}
            up = {k: pltpu.roll(t, SUBS - 1, 0) for k, t in tile.items()}
            for i in range(x_tiles):
                right = [pltpu.roll(tile[i, h], 1, 1) for h in range(2)]
                left = [pltpu.roll(tile[i, h], LANES - 1, 1) for h in range(2)]
                south = [jnp.where(first_lane, 0.0, right[0]), jnp.where(first_lane, *right)]
                north = [
                    jnp.where(last_lane, left[1], left[0]),
                    jnp.where(last_lane, 0.0, left[1]),
                ]
                for h in range(2):
                    at = (slice(SUBS * i, SUBS * (i + 1)), slice(LANES * h, LANES * (h + 1)))
                    m_west = jnp.where(first_sub, down[i - 1, h] if i else zero, down[i, h])
                    m_east = jnp.where(
                        last_sub, up[i + 1, h] if i + 1 < x_tiles else zero, up[i, h]
                    )
                    total = (centre_c[(z,) + at] - 6.0 * kappa) * tile[i, h]
                    total += (speed[(0, z) + at] + kappa) * air[(cur, f, z + 2) + at]
                    total += (in_z[(z,) + at] + kappa) * air[(cur, f, z) + at]
                    total += (speed[(1, z) + at] + kappa) * m_east
                    total += (in_x[(z,) + at] + kappa) * m_west
                    total += (speed[(2, z) + at] + kappa) * north[h]
                    total += (in_y[(z,) + at] + kappa) * south[h]
                    air[(new, f, z + 1) + at] = total

    def gather(s):
        cell = served[pl.ds(pl.multiple_of(s * ROWS, ROWS), ROWS), :][0:1].astype(I32)
        hot = col_hot[s]
        picked = dot(field_hi[...], hot) + dot(field_lo[...], hot)
        mask = lax.broadcasted_iota(I32, (rows, cap), 0) == cell // span
        return jnp.sum(jnp.where(mask, picked, 0.0), axis=0, keepdims=True)

    def scatter(step, s, fetched):
        at = pl.ds(pl.multiple_of(s * ROWS, ROWS), ROWS)
        wall = served[at, :]
        h = wall[1:2]
        half = RATIO * fetched * h
        flow = h * wall[2 + step : 3 + step] - half
        result[pl.ds(s * ROWS + step, 1), :] = flow
        if step + 1 < steps:
            later = [wall[k : k + 1] for k in range(3 + step)]
            for k in range(step + 1, steps):
                g = steps + k - step
                seen = half if k == step + 1 else half * wall[g : g + 1]
                later.append(wall[2 + k : 3 + k] + seen)
            later += [wall[k : k + 1] for k in range(2 + steps, ROWS)]
            served[at, :] = jnp.concatenate(later, axis=0)
        hi = flow.astype(BF16)
        lo = (flow - hi.astype(F32)).astype(BF16)
        hot = col_hot[s]
        where = row_hot[s]
        added[...] += dot_nt(where, hot * hi) + dot_nt(where, hot * lo)

    def return_copy(d):
        return parcel_copy(d, result, returned, return_send, return_recv)

    for step in range(steps):
        cur, new = step % 2, (step + 1) % 2
        last = step == steps - 1
        added[...] = jnp.zeros_like(added)

        def body(s, fetched, step=step, cur=cur, new=new):
            following = gather(lax.rem(s + 1, groups))
            scatter(step, s, fetched)
            return following

        lax.fori_loop(0, groups, body, gather(0))

        def body_z(z, carry, cur=cur, new=new):
            stencil(cur, new, z)
            return carry

        lax.fori_loop(0, depth, body_z, 0)

        if last:
            def send_back(d, carry):
                return_copy(d).start()
                return carry

            lax.fori_loop(1, groups, send_back, 0)
            own = pl.ds(pl.multiple_of(me * ROWS, ROWS), ROWS)
            returned[own, :] = result[own, :]

        for copy in halo_copies(step, cur):
            copy.wait()
        if step == 0:
            for copy in in_copies:
                copy.wait()
            in_z_halo[...] = in_z_halo[...] * has_below
            in_x_halo[...] = in_x_halo[...] * has_west
        for f in range(fields):
            kappa = kappa_ref[f]
            beyond = halo_z[step, 0, f] * has_below
            air[new, f, 1] += kappa * beyond + in_z_halo[...] * (beyond - air[cur, f, 1])
            beyond = halo_z[step, 1, f] * has_above
            air[new, f, depth] += (speed[0, depth - 1] + kappa) * beyond
            beyond = halo_x[step, 0, f] * has_west
            fix_x[0, f] = kappa * beyond + in_x_halo[...] * (beyond - edge_x[step, 0, f])
            beyond = halo_x[step, 1, f] * has_east
            fix_x[1, f] = (out_x_last[...] + kappa) * beyond

        def finish(z, carry, step=step, new=new, last=last):
            at = pl.ds(pl.multiple_of(z * breadth, breadth), breadth)
            air[new, 0, z + 1] += added[at, :]
            for f in range(fields):
                low = air[new, f, z + 1, 0:1, :] + fix_x[0, f, pl.ds(z, 1), :]
                high = (
                    air[new, f, z + 1, breadth - 1 : breadth, :] + fix_x[1, f, pl.ds(z, 1), :]
                )
                air[new, f, z + 1, 0:1, :] = low
                air[new, f, z + 1, breadth - 1 : breadth, :] = high
                if not last:
                    edge_x[step + 1, 0, f, pl.ds(z, 1), :] = low
                    edge_x[step + 1, 1, f, pl.ds(z, 1), :] = high
            if not last:
                split_plane(new, z)
            return carry

        lax.fori_loop(0, depth, finish, 0)
        if not last:
            for copy in halo_copies(step + 1, new):
                copy.start()

    store = pltpu.make_async_copy(
        air.at[steps % 2, :, pl.ds(1, depth)], air_out, store_sem
    )
    store.start()

    def wait_back(d, carry):
        return_copy(d).wait()
        return carry

    lax.fori_loop(1, groups, wait_back, 0)
    back = returned[...]
    placed = dot(jnp.concatenate(split(back, 3), axis=0).astype(BF16), rank_hot[...])
    placed = placed[:n] + placed[n : 2 * n] + placed[2 * n :]
    flows = jnp.zeros((ROWS, walls), F32)
    for b in range(groups):
        flows = flows + owned[b : b + 1] * placed[b * ROWS : (b + 1) * ROWS]
    p = wall_ref[...]
    grad = jnp.zeros((ROWS, walls), F32)
    for step in range(steps):
        saved = saved_ref[steps - 1 - step]
        grad = grad - (pltpu.roll(saved, ROWS - 1, 0) - saved) * (pltpu.roll(p, ROWS - 1, 0) - p)
        p = wall_back(p, cond8) - surface * flows[step : step + 1]
    wall_out[...] = p
    grad_out[...] = grad[: ROWS - 1]
    store.wait()


def per_device(
    air_seed,
    wall_seed,
    speed,
    upwind,
    diffusivity,
    conductivity,
    wall_saved,
    heat_table,
    interface,
    owner,
    material,
):
    groups, columns = lax.axis_size("vert"), lax.axis_size("horiz")
    steps = wall_saved.shape[0]
    walls = interface.shape[0]
    cap = walls // 4
    fields, depth, breadth, span = air_seed.shape
    rows = depth * breadth
    vmem = pl.BlockSpec(memory_space=pltpu.VMEM)
    smem = pl.BlockSpec(memory_space=pltpu.SMEM)
    hbm = pl.BlockSpec(memory_space=pl.ANY)
    dma = pltpu.SemaphoreType.DMA
    plane = (breadth, span)
    brick = (depth, breadth, span)
    side = (depth, span)
    scratch = [
        pltpu.VMEM((2, fields, depth + 2) + plane, F32),
        pltpu.VMEM((3,) + brick, F32),
        pltpu.VMEM((3,) + brick, I32),
        pltpu.VMEM((depth + 1,) + plane, F32),
        pltpu.VMEM(brick, F32),
        pltpu.VMEM(brick, F32),
        pltpu.VMEM(brick, F32),
        pltpu.VMEM(side, F32),
        pltpu.VMEM(side, F32),
        pltpu.VMEM(plane, F32),
        pltpu.VMEM(side, F32),
        pltpu.VMEM((steps, 2, fields) + plane, F32),
        pltpu.VMEM((steps, 2, fields) + side, F32),
        pltpu.VMEM((steps, 2, fields) + side, F32),
        pltpu.VMEM((2, fields) + side, F32),
        pltpu.VMEM((rows, span), BF16),
        pltpu.VMEM((rows, span), BF16),
        pltpu.VMEM((groups, rows, cap), BF16),
        pltpu.VMEM((groups, span, cap), BF16),
        pltpu.VMEM((rows, span), F32),
        pltpu.VMEM((3 * groups * ROWS, walls), BF16),
        pltpu.VMEM((cap, walls), BF16),
        pltpu.VMEM((groups * ROWS, cap), F32),
        pltpu.VMEM((groups * ROWS, cap), F32),
        pltpu.VMEM((groups * ROWS, cap), F32),
        pltpu.VMEM((groups * ROWS, cap), F32),
        dma((3,)),
        dma(()),
        dma((2,)),
        dma((2,)),
        dma((steps, 4)),
        dma((steps, 4)),
        dma((groups,)),
        dma((groups,)),
        dma((groups,)),
        dma((groups,)),
    ]
    return pl.pallas_call(
        functools.partial(kernel, (steps, groups, columns)),
        out_shape=(
            jax.ShapeDtypeStruct(air_seed.shape, F32),
            jax.ShapeDtypeStruct(wall_seed.shape, F32),
            jax.ShapeDtypeStruct(conductivity.shape, F32),
        ),
        in_specs=[smem, smem] + [vmem] * 6 + [hbm] * 3,
        out_specs=(hbm, vmem, vmem),
        scratch_shapes=scratch,
        compiler_params=pltpu.CompilerParams(
            collective_id=0, has_side_effects=True, vmem_limit_bytes=48 * 1024 * 1024
        ),
        cost_estimate=pl.CostEstimate(
            flops=2 * steps * 4 * groups * cap * rows * span,
            bytes_accessed=40 * rows * span,
            transcendentals=0,
        ),
    )(
        diffusivity,
        heat_table,
        wall_seed,
        conductivity,
        wall_saved,
        interface.reshape(1, walls),
        owner.reshape(1, walls),
        material.reshape(1, walls),
        air_seed,
        speed,
        upwind,
    )


def solution(mesh):
    air = P(None, "vert", "horiz", None)
    wall = P(None, ("horiz", "vert"))
    column = P(("horiz", "vert"))
    return jax.shard_map(
        per_device,
        mesh=mesh,
        in_specs=(
            air,
            wall,
            air,
            air,
            P(),
            wall,
            P(None, None, ("horiz", "vert")),
            P(),
            column,
            P(("horiz", "vert"), None),
            column,
        ),
        out_specs=(air, wall, wall),
        check_vma=False,
    )
```

profile of v0, /device:TPU:1, one launch (start us, length us, event | category | flops | bytes accessed | tf_op | source)
XLA Modules:
  0.0 77.7 jit_solution(11766751963778966536)
XLA Ops:
  0.6 0.0 copy-start
  0.6 1.4 %copy-done = f32[3,16,32,256]{3,2,1,0:T(8,128)S(1)} copy-done((f32[3,16,32,256]{3,2,1,0:T(8,128)S(1)}, f32[3,16,32,256]{3,2,1,0:T(8,128)}, u32[]{:S(2)}) %copy-start) | copy-done | bytes 1572888
  2.0 0.0 copy-start.1
  2.0 1.4 %copy-done.1 = s32[3,16,32,256]{3,2,1,0:T(8,128)S(1)} copy-done((s32[3,16,32,256]{3,2,1,0:T(8,128)S(1)}, s32[3,16,32,256]{3,2,1,0:T(8,128)}, u32[]{:S(2)}) %copy-start.1) | copy-done | bytes 1572888
  3.5 0.0 copy-start.2
  3.5 0.9 %copy-done.2 = f32[4,8,1024]{2,1,0:T(8,128)S(1)} copy-done((f32[4,8,1024]{2,1,0:T(8,128)S(1)}, f32[4,8,1024]{2,1,0:T(8,128)}, u32[]{:S(2)}) %copy-start.2) | copy-done | bytes 131096
  4.4 0.0 copy-start.3
  4.4 0.8 copy-done.3
  5.1 0.0 copy-start.4
  5.1 0.8 copy-done.4
  5.9 0.0 copy-start.5
  5.9 0.7 copy-done.5
  6.6 0.0 copy-start.6
  6.6 0.7 copy-done.6
  7.2 0.0 copy-start.7
  7.3 0.7 copy-done.7
  7.9 0.0 copy-start.8
  7.9 0.7 copy-done.8
  8.6 0.0 copy-start.9
  8.6 0.7 copy-done.9
  9.2 65.7 %shard_map.130 = (f32[5,16,32,256]{3,2,1,0:T(8,128)S(1)}, f32[8,1024]{1,0:T(8,128)S(1)}, f32[7,1024]{1,0:T(8,128)S(1)}) custom-call(f32[5]{0:T(128)S(1)} %copy-done.8, f32[8]{0:T(128)S(1)} %copy-done.9, f32[8,1024]{1,0:T(8,128)S(1)} %copy-done.3, f32[7,1024]{1,0:T(8,128)S(1)} %copy-done.4, f32[4,8,1024]{2,1,0:T(8,128)S(1)} %copy-done.2, ...), custom_call_target="tpu_custom_call" | custom-call | flops 17179869184 | bytes 5242880 | tf_op jit(solution)/shard_map/pallas_call | solution.py:539
  75.0 1.5 %copy.17 = f32[5,16,32,256]{3,2,1,0:T(8,128)} copy(f32[5,16,32,256]{3,2,1,0:T(8,128)S(1)} %get-tuple-element.6) | data formatting | bytes 5242880
  76.5 0.6 copy.18
  77.1 0.6 copy.19
Async XLA Ops:
  0.6 1.4 %copy-start = (f32[3,16,32,256]{3,2,1,0:T(8,128)S(1)}, f32[3,16,32,256]{3,2,1,0:T(8,128)}, u32[]{:S(2)}) copy-start(f32[3,16,32,256]{3,2,1,0:T(8,128)} %speed_hbm.1) | copy-start | bytes 4718596
  2.0 1.4 %copy-start.1 = (s32[3,16,32,256]{3,2,1,0:T(8,128)S(1)}, s32[3,16,32,256]{3,2,1,0:T(8,128)}, u32[]{:S(2)}) copy-start(s32[3,16,32,256]{3,2,1,0:T(8,128)} %upwind_hbm.1) | copy-start | bytes 4718596
  3.5 0.9 %copy-start.2 = (f32[4,8,1024]{2,1,0:T(8,128)S(1)}, f32[4,8,1024]{2,1,0:T(8,128)}, u32[]{:S(2)}) copy-start(f32[4,8,1024]{2,1,0:T(8,128)} %saved_ref.1) | copy-start | bytes 393220
  4.4 0.8 copy-start.3
  5.1 0.8 copy-start.4
  5.9 0.7 copy-start.5
  6.6 0.7 copy-start.6
  7.2 0.7 copy-start.7
  7.9 0.7 copy-start.8
  8.6 0.7 copy-start.9
where the time goes:
time: 78.1 us; the launch traced here: 77.7 us
  Pallas kernels  65.7 us (84%)
  local copies, waits for them, and re-layouts  11.3 us (14%)
    pallas_call x1, Pallas kernels, per_device(): pl.pallas_call(functools.partial(kernel, (steps, groups, columns)), out_s...  65.7 us
    unnamed x23, local copies, waits for them, and re-layouts  11.3 us

commit v1 on v0

v1 whole, which is shorter than its diff:
```python
import functools

import jax
import jax.numpy as jnp
from jax import lax
from jax.experimental import pallas as pl
from jax.experimental.pallas import tpu as pltpu
from jax.sharding import PartitionSpec as P

F32, BF16, I32 = jnp.float32, jnp.bfloat16, jnp.int32
MESH = pl.DeviceIdType.MESH
LANES, SUBS = 128, 8
RATIO = 0.5
VMEM_BYTES = 64 * 1024 * 1024 - 64 * 1024
ROWS = 8
NT = (((1,), (1,)), ((), ()))


def dot(a, b):
    return jnp.dot(a, b, preferred_element_type=F32)


def dot_nt(a, b):
    return lax.dot_general(a, b, NT, preferred_element_type=F32)


def split(value, parts):
    pieces = []
    for _ in range(parts):
        piece = value.astype(BF16).astype(F32)
        pieces.append(piece)
        value = value - piece
    return pieces


def wall_back(p, cond8):
    flux = cond8 * (pltpu.roll(p, ROWS - 1, 0) - p)
    return p + flux - pltpu.roll(flux, 1, 0)


def kernel(
    dims,
    kappa_ref,
    table_ref,
    wall_hbm,
    cond_hbm,
    saved_hbm,
    face_hbm,
    owner_hbm,
    mat_hbm,
    air_hbm,
    speed_hbm,
    upwind_hbm,
    air_out,
    wall_out,
    grad_out,
    wall_ref,
    cond_ref,
    saved_ref,
    face_ref,
    owner_ref,
    mat_ref,
    air,
    speed,
    upwind,
    in_z,
    in_x,
    in_y,
    centre_c,
    out_x_last,
    in_x_last,
    in_z_halo,
    in_x_halo,
    halo_z,
    halo_x,
    edge_x,
    fix_x,
    field_t,
    row_hot,
    col_hot,
    flows_ref,
    added,
    parts_ref,
    rank_hot,
    owned_ref,
    parcel,
    served,
    result,
    returned,
    wall_res,
    grad_res,
    load_sem,
    store_sem,
    in_send,
    in_recv,
    halo_send,
    halo_recv,
    parcel_send,
    parcel_recv,
    return_send,
    return_recv,
):
    steps, groups, columns = dims
    fields, depth, breadth, span = air_out.shape
    walls = face_ref.shape[1]
    cap = rank_hot.shape[0]
    rows = depth * breadth
    x_tiles = breadth // SUBS
    chunks, _, chunk = served.shape
    per_chunk = chunk // cap
    me = lax.axis_index("vert")
    col = lax.axis_index("horiz")
    above, below = lax.rem(me + 1, groups), lax.rem(me + groups - 1, groups)
    east, west = lax.rem(col + 1, columns), lax.rem(col + columns - 1, columns)
    has_below = jnp.where(me > 0, 1.0, 0.0).astype(F32)
    has_above = jnp.where(me < groups - 1, 1.0, 0.0).astype(F32)
    has_west = jnp.where(col > 0, 1.0, 0.0).astype(F32)
    has_east = jnp.where(col < columns - 1, 1.0, 0.0).astype(F32)

    barrier = pltpu.get_barrier_semaphore()

    def greet(d, carry):
        pl.semaphore_signal(
            barrier, inc=1, device_id={"vert": lax.rem(me + d, groups)}, device_id_type=MESH
        )
        return carry

    loads = [
        pltpu.make_async_copy(src, dst, load_sem.at[k])
        for k, (src, dst) in enumerate(
            [
                (owner_hbm, owner_ref),
                (face_hbm, face_ref),
                (mat_hbm, mat_ref),
                (wall_hbm, wall_ref),
                (cond_hbm, cond_ref),
                (air_hbm, air.at[0, :, pl.ds(1, depth)]),
                (speed_hbm, speed),
                (upwind_hbm, upwind),
                (saved_hbm, saved_ref),
            ]
        )
    ]
    for load in loads:
        load.start()
    lax.fori_loop(1, groups, greet, 0)
    for neighbour in (east, west):
        pl.semaphore_signal(barrier, inc=1, device_id={"horiz": neighbour}, device_id_type=MESH)

    plane0 = jnp.zeros((fields, breadth, span), F32)
    for slot in range(2):
        air[slot, :, 0] = plane0
        air[slot, :, depth + 1] = plane0
    in_z[0] = jnp.zeros((breadth, span), F32)
    result[...] = jnp.zeros_like(result)

    loads[0].wait()
    owned = (lax.broadcasted_iota(I32, (groups, walls), 0) == owner_ref[...]).astype(F32)
    owned_ref[...] = owned
    block = 2 * LANES
    blocks = walls // block
    stacked = jnp.concatenate(
        [owned[:, k * block : (k + 1) * block] for k in range(blocks)], axis=0
    )
    lower = (
        lax.broadcasted_iota(I32, (block, block), 0) < lax.broadcasted_iota(I32, (block, block), 1)
    ).astype(F32)
    before = dot(stacked.astype(BF16), lower.astype(BF16))
    totals = jnp.sum(stacked, axis=1, keepdims=True)
    offset = jnp.zeros((groups, 1), F32)
    ranks = []
    for k in range(blocks):
        part = slice(k * groups, (k + 1) * groups)
        ranks.append(
            jnp.sum(stacked[part] * (before[part] + offset), axis=0, keepdims=True)
        )
        offset = offset + totals[part]
    ranks = jnp.concatenate(ranks, axis=1).astype(I32)
    rank_hot[...] = (
        (lax.broadcasted_iota(I32, (cap, walls), 0) == ranks).astype(F32).astype(BF16)
    )

    for load in loads[1:5]:
        load.wait()
    material = mat_ref[...]
    hcoef = jnp.zeros(material.shape, F32)
    for k in range(table_ref.shape[0]):
        hcoef = jnp.where(material == k, table_ref[k], hcoef)
    layer = lax.broadcasted_iota(I32, (ROWS, walls), 0)
    surface = (layer == 0).astype(F32)
    cond8 = jnp.concatenate([cond_ref[...], jnp.zeros((1, walls), F32)], axis=0)
    h_top = surface * hcoef
    p = wall_ref[...]
    e = surface
    values = [face_ref[...].astype(F32), hcoef]
    for step in range(steps):
        values.append(p[0:1])
        if step < steps - 1:
            p = wall_back(p, cond8) - h_top * p
    for _ in range(steps - 2):
        e = wall_back(e, cond8) - h_top * e
        values.append(e[0:1])
    values = jnp.concatenate(values, axis=0)
    for s, piece in enumerate(split(values, 3)):
        for b in range(0, groups, 2):
            pair = jnp.concatenate([piece * owned[b : b + 1], piece * owned[b + 1 : b + 2]], axis=0)
            parts_ref[pl.ds((s * groups + b) * ROWS, 2 * ROWS), :] = pair.astype(BF16)
    placed = dot_nt(parts_ref[...], rank_hot[...])
    n = groups * ROWS
    parcel[...] = placed[:n] + placed[n : 2 * n] + placed[2 * n :]

    def at_rows(k):
        return pl.ds(pl.multiple_of(k * ROWS, ROWS), ROWS)

    def at_lanes(k):
        return pl.ds(pl.multiple_of(lax.rem(k, per_chunk) * cap, cap), cap)

    served[lax.div(me, per_chunk), :, at_lanes(me)] = parcel[at_rows(me), :]

    pl.semaphore_wait(barrier, groups + 1)

    def parcel_copy(d):
        to = lax.rem(me + d, groups)
        return pltpu.make_async_remote_copy(
            src_ref=parcel.at[at_rows(to)],
            dst_ref=served.at[lax.div(me, per_chunk), :, at_lanes(me)],
            send_sem=parcel_send.at[d],
            recv_sem=parcel_recv.at[d],
            device_id={"vert": to},
            device_id_type=MESH,
        )

    def return_copy(d):
        to = lax.rem(me + d, groups)
        return pltpu.make_async_remote_copy(
            src_ref=result.at[lax.div(to, per_chunk), :, at_lanes(to)],
            dst_ref=returned.at[at_rows(me)],
            send_sem=return_send.at[d],
            recv_sem=return_recv.at[d],
            device_id={"vert": to},
            device_id_type=MESH,
        )

    def each(copy, act):
        def body(d, carry):
            act(copy(d))
            return carry

        lax.fori_loop(1, groups, body, 0)

    each(parcel_copy, lambda copy: copy.start())

    def halo_copies(step, slot):
        return [
            pltpu.make_async_remote_copy(
                src_ref=src,
                dst_ref=dst,
                send_sem=halo_send.at[step, k],
                recv_sem=halo_recv.at[step, k],
                device_id=to,
                device_id_type=MESH,
            )
            for k, (src, dst, to) in enumerate(
                [
                    (air.at[slot, :, depth], halo_z.at[step, 0], {"vert": above}),
                    (air.at[slot, :, 1], halo_z.at[step, 1], {"vert": below}),
                    (edge_x.at[step, 1], halo_x.at[step, 0], {"horiz": east}),
                    (edge_x.at[step, 0], halo_x.at[step, 1], {"horiz": west}),
                ]
            )
        ]

    planes = LANES // breadth

    def split_field(slot):
        def body(k, carry):
            block = air[slot, 0, pl.ds(1 + k * planes, planes)].reshape(LANES, span).T
            hi = block.astype(BF16)
            field_t[:, pl.ds(pl.multiple_of(k * LANES, LANES), LANES)] = hi
            field_t[:, pl.ds(pl.multiple_of(rows + k * LANES, LANES), LANES)] = (
                block - hi.astype(F32)
            ).astype(BF16)
            return carry

        lax.fori_loop(0, depth // planes, body, 0)

    loads[5].wait()

    def pack_first(z, carry):
        for f in range(fields):
            edge_x[0, 0, f, pl.ds(z, 1), :] = air[0, f, z + 1, 0:1, :]
            edge_x[0, 1, f, pl.ds(z, 1), :] = air[0, f, z + 1, breadth - 1 : breadth, :]
        return carry

    lax.fori_loop(0, depth, pack_first, 0)
    for copy in halo_copies(0, 0):
        copy.start()
    split_field(0)

    loads[6].wait()
    loads[7].wait()
    row_id = lax.broadcasted_iota(I32, (breadth, span), 0)
    lane_id = lax.broadcasted_iota(I32, (breadth, span), 1)

    def coefficients(z, carry):
        out, inn = [], []
        for d in range(3):
            s = speed[d, z]
            o = s * upwind[d, z].astype(F32)
            out.append(o)
            inn.append(s - o)
            speed[d, z] = o
        in_z[z + 1] = -inn[0]
        in_x_last[pl.ds(z, 1), :] = -inn[1][breadth - 1 : breadth]
        out_x_last[pl.ds(z, 1), :] = out[1][breadth - 1 : breadth]
        low_x = jnp.where(row_id == 0, 0.0, pltpu.roll(-inn[1], 1, 0))
        low_y = jnp.where(lane_id == 0, 0.0, pltpu.roll(-inn[2], 1, 1))
        in_x[z] = low_x
        in_y[z] = low_y
        centre_c[z] = 1.0 - (out[0] + out[1] + out[2]) - (in_z[z] + low_x + low_y)
        return carry

    lax.fori_loop(0, depth, coefficients, 0)
    in_copies = [
        pltpu.make_async_remote_copy(
            src_ref=src,
            dst_ref=dst,
            send_sem=in_send.at[k],
            recv_sem=in_recv.at[k],
            device_id=to,
            device_id_type=MESH,
        )
        for k, (src, dst, to) in enumerate(
            [
                (in_z.at[depth], in_z_halo, {"vert": above}),
                (in_x_last, in_x_halo, {"horiz": east}),
            ]
        )
    ]
    for copy in in_copies:
        copy.start()

    sub8 = lax.broadcasted_iota(I32, (SUBS, LANES), 0)
    lane8 = lax.broadcasted_iota(I32, (SUBS, LANES), 1)

    def stencil(cur, new, z):
        zero = jnp.zeros((SUBS, LANES), F32)
        first_lane, last_lane = lane8 == 0, lane8 == LANES - 1
        first_sub, last_sub = sub8 == 0, sub8 == SUBS - 1
        for f in range(fields):
            kappa = kappa_ref[f]
            tile = {}
            for i in range(x_tiles):
                for h in range(2):
                    tile[i, h] = air[
                        cur, f, z + 1, SUBS * i : SUBS * (i + 1), LANES * h : LANES * (h + 1)
                    ]
            down = {k: pltpu.roll(t, 1, 0) for k, t in tile.items()}
            up = {k: pltpu.roll(t, SUBS - 1, 0) for k, t in tile.items()}
            for i in range(x_tiles):
                right = [pltpu.roll(tile[i, h], 1, 1) for h in range(2)]
                left = [pltpu.roll(tile[i, h], LANES - 1, 1) for h in range(2)]
                south = [jnp.where(first_lane, 0.0, right[0]), jnp.where(first_lane, *right)]
                north = [
                    jnp.where(last_lane, left[1], left[0]),
                    jnp.where(last_lane, 0.0, left[1]),
                ]
                for h in range(2):
                    at = (slice(SUBS * i, SUBS * (i + 1)), slice(LANES * h, LANES * (h + 1)))
                    m_west = jnp.where(first_sub, down[i - 1, h] if i else zero, down[i, h])
                    m_east = jnp.where(
                        last_sub, up[i + 1, h] if i + 1 < x_tiles else zero, up[i, h]
                    )
                    total = (centre_c[(z,) + at] - 6.0 * kappa) * tile[i, h]
                    total += (speed[(0, z) + at] + kappa) * air[(cur, f, z + 2) + at]
                    total += (in_z[(z,) + at] + kappa) * air[(cur, f, z) + at]
                    total += (speed[(1, z) + at] + kappa) * m_east
                    total += (in_x[(z,) + at] + kappa) * m_west
                    total += (speed[(2, z) + at] + kappa) * north[h]
                    total += (in_y[(z,) + at] + kappa) * south[h]
                    air[(new, f, z + 1) + at] = total

    def stencil_first(z, carry):
        stencil(0, 1, z)
        return carry

    lax.fori_loop(0, depth, stencil_first, 0)
    each(parcel_copy, lambda copy: copy.wait())

    def one_hots(c, carry):
        cell = served[c, 0:1, :].astype(I32)
        hot = (lax.broadcasted_iota(I32, (rows, chunk), 0) == cell // span).astype(F32).astype(BF16)
        row_hot[c, :rows] = hot
        row_hot[c, rows:] = hot
        col_hot[c] = (
            (lax.broadcasted_iota(I32, (span, chunk), 0) == cell % span).astype(F32).astype(BF16)
        )
        return carry

    lax.fori_loop(0, chunks, one_hots, 0)

    def gather(step, c):
        picked = dot(field_t[...], row_hot[c])
        wall = served[c]
        y = wall[0:1].astype(I32) % span
        mask = lax.broadcasted_iota(I32, (span, chunk), 0) == y
        fetched = jnp.sum(jnp.where(mask, picked, 0.0), axis=0, keepdims=True)
        h = wall[1:2]
        half = RATIO * fetched * h
        flow = h * wall[2 + step : 3 + step] - half
        flows_ref[pl.ds(c, 1), :] = flow
        result[c, step : step + 1, :] = flow
        if step + 1 < steps:
            later = [wall[k : k + 1] for k in range(3 + step)]
            for k in range(step + 1, steps):
                g = steps + k - step
                seen = half if k == step + 1 else half * wall[g : g + 1]
                later.append(wall[2 + k : 3 + k] + seen)
            later += [wall[k : k + 1] for k in range(2 + steps, ROWS)]
            served[c] = jnp.concatenate(later, axis=0)

    def scatter(c):
        flow = flows_ref[pl.ds(c, 1), :]
        hi = flow.astype(BF16)
        lo = (flow - hi.astype(F32)).astype(BF16)
        hot = col_hot[c]
        where = row_hot[c, :rows]
        added[...] += dot_nt(where, hot * hi) + dot_nt(where, hot * lo)

    def beyond_z(step, f):
        cur, new = step % 2, (step + 1) % 2
        kappa = kappa_ref[f]
        beyond = halo_z[step, 0, f] * has_below
        air[new, f, 1] += kappa * beyond + in_z_halo[...] * (beyond - air[cur, f, 1])
        beyond = halo_z[step, 1, f] * has_above
        air[new, f, depth] += (speed[0, depth - 1] + kappa) * beyond
        beyond = halo_x[step, 0, f] * has_west
        fix_x[0, f] = kappa * beyond + in_x_halo[...] * (beyond - edge_x[step, 0, f])
        beyond = halo_x[step, 1, f] * has_east
        fix_x[1, f] = (out_x_last[...] + kappa) * beyond

    def finish(step, chosen):
        new = (step + 1) % 2
        for f in chosen:
            beyond_z(step, f)

        def body(z, carry):
            at = pl.ds(pl.multiple_of(z * breadth, breadth), breadth)
            if 0 in chosen:
                air[new, 0, z + 1] += added[at, :]
            for f in chosen:
                low = air[new, f, z + 1, 0:1, :] + fix_x[0, f, pl.ds(z, 1), :]
                high = (
                    air[new, f, z + 1, breadth - 1 : breadth, :] + fix_x[1, f, pl.ds(z, 1), :]
                )
                air[new, f, z + 1, 0:1, :] = low
                air[new, f, z + 1, breadth - 1 : breadth, :] = high
                if step + 1 < steps:
                    edge_x[step + 1, 0, f, pl.ds(z, 1), :] = low
                    edge_x[step + 1, 1, f, pl.ds(z, 1), :] = high
            return carry

        lax.fori_loop(0, depth, body, 0)

    def wait_halos(step):
        for copy in halo_copies(step, step % 2):
            copy.wait()
        if step == 0:
            for copy in in_copies:
                copy.wait()
            in_z_halo[...] = in_z_halo[...] * has_below
            in_x_halo[...] = in_x_halo[...] * has_west

    def store(f):
        return pltpu.make_async_copy(
            air.at[steps % 2, f, pl.ds(1, depth)], air_out.at[f], store_sem.at[f]
        )

    for step in range(steps):
        cur, new = step % 2, (step + 1) % 2
        last = step == steps - 1
        in_gather = 0 if step == 0 else depth // chunks if last else depth // chunks // 2
        in_scatter = 0 if step == 0 else depth // chunks - in_gather

        def body_gather(c, carry, step=step, cur=cur, new=new, count=in_gather):
            gather(step, c)
            for k in range(count):
                stencil(cur, new, c * count + k)
            return carry

        lax.fori_loop(0, chunks, body_gather, 0)
        if last:
            each(return_copy, lambda copy: copy.start())
            returned[at_rows(me), :] = result[lax.div(me, per_chunk), :, at_lanes(me)]
            wait_halos(step)
            finish(step, range(1, fields))
            for f in range(1, fields):
                store(f).start()
        added[...] = jnp.zeros_like(added)

        def body_scatter(c, carry, cur=cur, new=new, count=in_scatter, first=in_gather * chunks):
            scatter(c)
            for k in range(count):
                stencil(cur, new, first + c * count + k)
            return carry

        lax.fori_loop(0, chunks, body_scatter, 0)
        if last:
            finish(step, range(1))
            store(0).start()
        else:
            wait_halos(step)
            finish(step, range(fields))
            for copy in halo_copies(step + 1, new):
                copy.start()
            split_field(new)

    each(return_copy, lambda copy: copy.wait())
    loads[8].wait()
    placed = dot(jnp.concatenate(split(returned[...], 3), axis=0).astype(BF16), rank_hot[...])
    placed = placed[:n] + placed[n : 2 * n] + placed[2 * n :]
    flows = jnp.zeros((ROWS, walls), F32)
    for b in range(groups):
        flows = flows + owned_ref[b : b + 1] * placed[b * ROWS : (b + 1) * ROWS]
    p = wall_ref[...]
    cond8 = jnp.concatenate([cond_ref[...], jnp.zeros((1, walls), F32)], axis=0)
    grad = jnp.zeros((ROWS, walls), F32)
    for step in range(steps):
        saved = saved_ref[steps - 1 - step]
        grad = grad - (pltpu.roll(saved, ROWS - 1, 0) - saved) * (pltpu.roll(p, ROWS - 1, 0) - p)
        p = wall_back(p, cond8) - surface * flows[step : step + 1]
    wall_res[...] = p
    grad_res[...] = grad[: ROWS - 1]
    stores = [
        pltpu.make_async_copy(wall_res, wall_out, store_sem.at[fields]),
        pltpu.make_async_copy(grad_res, grad_out, store_sem.at[fields + 1]),
    ]
    for copy in stores:
        copy.start()
    for copy in stores + [store(f) for f in range(fields)]:
        copy.wait()


def per_device(
    air_seed,
    wall_seed,
    speed,
    upwind,
    diffusivity,
    conductivity,
    wall_saved,
    heat_table,
    interface,
    owner,
    material,
):
    groups, columns = lax.axis_size("vert"), lax.axis_size("horiz")
    steps = wall_saved.shape[0]
    walls = interface.shape[0]
    cap = walls // 4
    fields, depth, breadth, span = air_seed.shape
    rows = depth * breadth
    chunks = 2
    chunk = groups * cap // chunks
    smem = pl.BlockSpec(memory_space=pltpu.SMEM)
    hbm = pl.BlockSpec(memory_space=pl.ANY)
    dma = pltpu.SemaphoreType.DMA
    plane = (breadth, span)
    brick = (depth, breadth, span)
    side = (depth, span)
    scratch = [
        pltpu.VMEM(wall_seed.shape, F32),
        pltpu.VMEM(conductivity.shape, F32),
        pltpu.VMEM(wall_saved.shape, F32),
        pltpu.VMEM((1, walls), I32),
        pltpu.VMEM((1, walls), I32),
        pltpu.VMEM((1, walls), I32),
        pltpu.VMEM((2, fields, depth + 2) + plane, F32),
        pltpu.VMEM((3,) + brick, F32),
        pltpu.VMEM((3,) + brick, I32),
        pltpu.VMEM((depth + 1,) + plane, F32),
        pltpu.VMEM(brick, F32),
        pltpu.VMEM(brick, F32),
        pltpu.VMEM(brick, F32),
        pltpu.VMEM(side, F32),
        pltpu.VMEM(side, F32),
        pltpu.VMEM(plane, F32),
        pltpu.VMEM(side, F32),
        pltpu.VMEM((steps, 2, fields) + plane, F32),
        pltpu.VMEM((steps, 2, fields) + side, F32),
        pltpu.VMEM((steps, 2, fields) + side, F32),
        pltpu.VMEM((2, fields) + side, F32),
        pltpu.VMEM((span, 2 * rows), BF16),
        pltpu.VMEM((chunks, 2 * rows, chunk), BF16),
        pltpu.VMEM((chunks, span, chunk), BF16),
        pltpu.VMEM((chunks, chunk), F32),
        pltpu.VMEM((rows, span), F32),
        pltpu.VMEM((3 * groups * ROWS, walls), BF16),
        pltpu.VMEM((cap, walls), BF16),
        pltpu.VMEM((groups, walls), F32),
        pltpu.VMEM((groups * ROWS, cap), F32),
        pltpu.VMEM((chunks, ROWS, chunk), F32),
        pltpu.VMEM((chunks, ROWS, chunk), F32),
        pltpu.VMEM((groups * ROWS, cap), F32),
        pltpu.VMEM(wall_seed.shape, F32),
        pltpu.VMEM(conductivity.shape, F32),
        dma((9,)),
        dma((fields + 2,)),
        dma((2,)),
        dma((2,)),
        dma((steps, 4)),
        dma((steps, 4)),
        dma((groups,)),
        dma((groups,)),
        dma((groups,)),
        dma((groups,)),
    ]
    return pl.pallas_call(
        functools.partial(kernel, (steps, groups, columns)),
        out_shape=(
            jax.ShapeDtypeStruct(air_seed.shape, F32),
            jax.ShapeDtypeStruct(wall_seed.shape, F32),
            jax.ShapeDtypeStruct(conductivity.shape, F32),
        ),
        in_specs=[smem, smem] + [hbm] * 9,
        out_specs=(hbm, hbm, hbm),
        scratch_shapes=scratch,
        compiler_params=pltpu.CompilerParams(
            collective_id=0, has_side_effects=True, vmem_limit_bytes=VMEM_BYTES
        ),
        cost_estimate=pl.CostEstimate(
            flops=2 * steps * 4 * groups * cap * rows * span,
            bytes_accessed=40 * rows * span,
            transcendentals=0,
        ),
    )(
        diffusivity,
        heat_table,
        wall_seed,
        conductivity,
        wall_saved,
        interface.reshape(1, walls),
        owner.reshape(1, walls),
        material.reshape(1, walls),
        air_seed,
        speed,
        upwind,
    )


def solution(mesh):
    air = P(None, "vert", "horiz", None)
    wall = P(None, ("horiz", "vert"))
    column = P(("horiz", "vert"))
    return jax.shard_map(
        per_device,
        mesh=mesh,
        in_specs=(
            air,
            wall,
            air,
            air,
            P(),
            wall,
            P(None, None, ("horiz", "vert")),
            P(),
            column,
            P(("horiz", "vert"), None),
            column,
        ),
        out_specs=(air, wall, wall),
        check_vma=False,
    )
```

time: 78.1 us -> 60.5 us (0.77)
  Pallas kernels: 65.7 us -> 54.8 us
  local copies, waits for them, and re-layouts: 11.3 us -> 4.81 us
    pallas_call x1, Pallas kernels: 65.7 us -> 54.8 us  [per_device(): pl.pallas_call(functools.partial(kernel, (steps, groups, columns)), out_s...]
    unnamed x23 -> x7, local copies, waits for them, and re-layouts: 11.3 us -> 4.81 us
where the time goes in v1:
time: 60.5 us; the launch traced here: 60.3 us
  Pallas kernels  54.8 us (91%)
  local copies, waits for them, and re-layouts  4.81 us (8%)
  between operations  0.66 us (1%)
    pallas_call x1, Pallas kernels, per_device(): pl.pallas_call(functools.partial(kernel, (steps, groups, columns)), out_s...  54.8 us
    unnamed x7, local copies, waits for them, and re-layouts  4.81 us

profile of v1, /device:TPU:1, one launch (start us, length us, event | category | flops | bytes accessed | tf_op | source)
XLA Modules:
  0.0 60.3 jit_solution(12637753667667219334)
XLA Ops:
  0.6 54.8 %shard_map.130 = (f32[5,16,32,256]{3,2,1,0:T(8,128)}, f32[8,1024]{1,0:T(8,128)}, f32[7,1024]{1,0:T(8,128)}) custom-call(f32[5]{0:T(128)} %kappa_ref.1, f32[8]{0:T(128)} %table_ref.1, f32[8,1024]{1,0:T(8,128)} %wall_hbm.1, f32[7,1024]{1,0:T(8,128)} %cond_hbm.1, f32[4,8,1024]{2,1,0:T(8,128)} %saved_hbm.1, s32[1,1024]{1,0:T(1,128)} %bitcast.3, ...), custom_call_target="tpu_custom_call" | custom-call | flops 17179869184 | bytes 5242880 | tf_op jit(solution)/shard_map/pallas_call | solution.py:618
  55.5 0.0 copy-start.1
  55.5 0.0 copy-start
  55.5 3.6 %copy.17 = f32[5,16,32,256]{3,2,1,0:T(8,128)} copy(f32[5,16,32,256]{3,2,1,0:T(8,128)} %get-tuple-element.6) | data formatting | bytes 5242880
  59.1 0.0 copy-done.1
  59.1 0.6 %copy.18 = f32[8,1024]{1,0:T(8,128)} copy(f32[8,1024]{1,0:T(8,128)S(1)} %copy-done.1) | data formatting | bytes 65536
  59.7 0.0 copy-done
  59.7 0.6 %copy.19 = f32[7,1024]{1,0:T(8,128)} copy(f32[7,1024]{1,0:T(8,128)S(1)} %copy-done) | data formatting | bytes 57344
Async XLA Ops:
  55.5 3.6 %copy-start.1 = (f32[8,1024]{1,0:T(8,128)S(1)}, f32[8,1024]{1,0:T(8,128)}, u32[]{:S(2)}) copy-start(f32[8,1024]{1,0:T(8,128)} %get-tuple-element.7) | copy-start | bytes 98308
  55.5 4.2 %copy-start = (f32[7,1024]{1,0:T(8,128)S(1)}, f32[7,1024]{1,0:T(8,128)}, u32[]{:S(2)}) copy-start(f32[7,1024]{1,0:T(8,128)} %get-tuple-element.8) | copy-start | bytes 86020

commit v2 on v1

--- a/solution.py
+++ b/solution.py
@@ -11,6 +11,7 @@
 MESH = pl.DeviceIdType.MESH
 LANES, SUBS = 128, 8
 RATIO = 0.5
+UNROLL = 2
 VMEM_BYTES = 64 * 1024 * 1024 - 64 * 1024
 ROWS = 8
 NT = (((1,), (1,)), ((), ()))
@@ -44,7 +45,6 @@
     table_ref,
     wall_hbm,
     cond_hbm,
-    saved_hbm,
     face_hbm,
     owner_hbm,
     mat_hbm,
@@ -52,15 +52,15 @@
     speed_hbm,
     upwind_hbm,
     air_out,
-    wall_out,
-    grad_out,
+    returned_out,
+    ranks_out,
     wall_ref,
     cond_ref,
-    saved_ref,
     face_ref,
     owner_ref,
     mat_ref,
-    air,
+    air_even,
+    air_odd,
     speed,
     upwind,
     in_z,
@@ -82,13 +82,11 @@
     added,
     parts_ref,
     rank_hot,
-    owned_ref,
+    ranks_ref,
     parcel,
     served,
     result,
     returned,
-    wall_res,
-    grad_res,
     load_sem,
     store_sem,
     in_send,
@@ -101,6 +99,7 @@
     return_recv,
 ):
     steps, groups, columns = dims
+    airs = (air_even, air_odd)
     fields, depth, breadth, span = air_out.shape
     walls = face_ref.shape[1]
     cap = rank_hot.shape[0]
@@ -134,10 +133,9 @@
                 (mat_hbm, mat_ref),
                 (wall_hbm, wall_ref),
                 (cond_hbm, cond_ref),
-                (air_hbm, air.at[0, :, pl.ds(1, depth)]),
+                (air_hbm, air_even.at[:, pl.ds(1, depth)]),
                 (speed_hbm, speed),
                 (upwind_hbm, upwind),
-                (saved_hbm, saved_ref),
             ]
         )
     ]
@@ -148,15 +146,14 @@
         pl.semaphore_signal(barrier, inc=1, device_id={"horiz": neighbour}, device_id_type=MESH)
 
     plane0 = jnp.zeros((fields, breadth, span), F32)
-    for slot in range(2):
-        air[slot, :, 0] = plane0
-        air[slot, :, depth + 1] = plane0
+    for air in airs:
+        air[:, 0] = plane0
+        air[:, depth + 1] = plane0
     in_z[0] = jnp.zeros((breadth, span), F32)
     result[...] = jnp.zeros_like(result)
 
     loads[0].wait()
     owned = (lax.broadcasted_iota(I32, (groups, walls), 0) == owner_ref[...]).astype(F32)
-    owned_ref[...] = owned
     block = 2 * LANES
     blocks = walls // block
     stacked = jnp.concatenate(
@@ -176,6 +173,7 @@
         )
         offset = offset + totals[part]
     ranks = jnp.concatenate(ranks, axis=1).astype(I32)
+    ranks_ref[...] = ranks
     rank_hot[...] = (
         (lax.broadcasted_iota(I32, (cap, walls), 0) == ranks).astype(F32).astype(BF16)
     )
@@ -250,31 +248,40 @@
 
     each(parcel_copy, lambda copy: copy.start())
 
-    def halo_copies(step, slot):
+    def halo_copies(step, air, first, count, group):
+        some = pl.ds(first, count)
         return [
             pltpu.make_async_remote_copy(
                 src_ref=src,
                 dst_ref=dst,
-                send_sem=halo_send.at[step, k],
-                recv_sem=halo_recv.at[step, k],
+                send_sem=halo_send.at[step, group, k],
+                recv_sem=halo_recv.at[step, group, k],
                 device_id=to,
                 device_id_type=MESH,
             )
             for k, (src, dst, to) in enumerate(
                 [
-                    (air.at[slot, :, depth], halo_z.at[step, 0], {"vert": above}),
-                    (air.at[slot, :, 1], halo_z.at[step, 1], {"vert": below}),
-                    (edge_x.at[step, 1], halo_x.at[step, 0], {"horiz": east}),
-                    (edge_x.at[step, 0], halo_x.at[step, 1], {"horiz": west}),
+                    (air.at[some, depth], halo_z.at[step, 0, some], {"vert": above}),
+                    (air.at[some, 1], halo_z.at[step, 1, some], {"vert": below}),
+                    (edge_x.at[step, 1, some], halo_x.at[step, 0, some], {"horiz": east}),
+                    (edge_x.at[step, 0, some], halo_x.at[step, 1, some], {"horiz": west}),
                 ]
             )
         ]
 
+    pairs = halo_recv.shape[1] - 1
+    paired = (fields - 1) // pairs
+
+    def halos_of(step, air, group):
+        if isinstance(group, int) and group == pairs:
+            return halo_copies(step, air, 0, 1, pairs)
+        return halo_copies(step, air, 1 + group * paired, paired, group)
+
     planes = LANES // breadth
 
-    def split_field(slot):
+    def split_field(air):
         def body(k, carry):
-            block = air[slot, 0, pl.ds(1 + k * planes, planes)].reshape(LANES, span).T
+            block = air[0, pl.ds(1 + k * planes, planes)].reshape(LANES, span).T
             hi = block.astype(BF16)
             field_t[:, pl.ds(pl.multiple_of(k * LANES, LANES), LANES)] = hi
             field_t[:, pl.ds(pl.multiple_of(rows + k * LANES, LANES), LANES)] = (
@@ -282,20 +289,22 @@
             ).astype(BF16)
             return carry
 
-        lax.fori_loop(0, depth // planes, body, 0)
+        for k in range(depth // planes):
+            body(k, 0)
 
     loads[5].wait()
 
     def pack_first(z, carry):
         for f in range(fields):
-            edge_x[0, 0, f, pl.ds(z, 1), :] = air[0, f, z + 1, 0:1, :]
-            edge_x[0, 1, f, pl.ds(z, 1), :] = air[0, f, z + 1, breadth - 1 : breadth, :]
+            edge_x[0, 0, f, pl.ds(z, 1), :] = air_even[f, z + 1, 0:1, :]
+            edge_x[0, 1, f, pl.ds(z, 1), :] = air_even[f, z + 1, breadth - 1 : breadth, :]
         return carry
 
     lax.fori_loop(0, depth, pack_first, 0)
-    for copy in halo_copies(0, 0):
-        copy.start()
-    split_field(0)
+    for group in range(pairs + 1):
+        for copy in halos_of(0, air_even, group):
+            copy.start()
+    split_field(air_even)
 
     loads[6].wait()
     loads[7].wait()
@@ -343,17 +352,17 @@
     sub8 = lax.broadcasted_iota(I32, (SUBS, LANES), 0)
     lane8 = lax.broadcasted_iota(I32, (SUBS, LANES), 1)
 
-    def stencil(cur, new, z):
+    def stencil(cur, new, z, chosen):
         zero = jnp.zeros((SUBS, LANES), F32)
         first_lane, last_lane = lane8 == 0, lane8 == LANES - 1
         first_sub, last_sub = sub8 == 0, sub8 == SUBS - 1
-        for f in range(fields):
+        for f in chosen:
             kappa = kappa_ref[f]
             tile = {}
             for i in range(x_tiles):
                 for h in range(2):
-                    tile[i, h] = air[
-                        cur, f, z + 1, SUBS * i : SUBS * (i + 1), LANES * h : LANES * (h + 1)
+                    tile[i, h] = cur[
+                        f, z + 1, SUBS * i : SUBS * (i + 1), LANES * h : LANES * (h + 1)
                     ]
             down = {k: pltpu.roll(t, 1, 0) for k, t in tile.items()}
             up = {k: pltpu.roll(t, SUBS - 1, 0) for k, t in tile.items()}
@@ -372,19 +381,14 @@
                         last_sub, up[i + 1, h] if i + 1 < x_tiles else zero, up[i, h]
                     )
                     total = (centre_c[(z,) + at] - 6.0 * kappa) * tile[i, h]
-                    total += (speed[(0, z) + at] + kappa) * air[(cur, f, z + 2) + at]
-                    total += (in_z[(z,) + at] + kappa) * air[(cur, f, z) + at]
+                    total += (speed[(0, z) + at] + kappa) * cur[(f, z + 2) + at]
+                    total += (in_z[(z,) + at] + kappa) * cur[(f, z) + at]
                     total += (speed[(1, z) + at] + kappa) * m_east
                     total += (in_x[(z,) + at] + kappa) * m_west
                     total += (speed[(2, z) + at] + kappa) * north[h]
                     total += (in_y[(z,) + at] + kappa) * south[h]
-                    air[(new, f, z + 1) + at] = total
-
-    def stencil_first(z, carry):
-        stencil(0, 1, z)
-        return carry
-
-    lax.fori_loop(0, depth, stencil_first, 0)
+                    new[(f, z + 1) + at] = total
+
     each(parcel_copy, lambda copy: copy.wait())
 
     def one_hots(c, carry):
@@ -407,17 +411,16 @@
         fetched = jnp.sum(jnp.where(mask, picked, 0.0), axis=0, keepdims=True)
         h = wall[1:2]
         half = RATIO * fetched * h
-        flow = h * wall[2 + step : 3 + step] - half
+        flow = h * wall[2:3] - half
         flows_ref[pl.ds(c, 1), :] = flow
-        result[c, step : step + 1, :] = flow
-        if step + 1 < steps:
-            later = [wall[k : k + 1] for k in range(3 + step)]
-            for k in range(step + 1, steps):
-                g = steps + k - step
-                seen = half if k == step + 1 else half * wall[g : g + 1]
-                later.append(wall[2 + k : 3 + k] + seen)
-            later += [wall[k : k + 1] for k in range(2 + steps, ROWS)]
-            served[c] = jnp.concatenate(later, axis=0)
+        result[c, pl.ds(step, 1), :] = flow
+        later = [wall[0:1], h, wall[3:4] + half]
+        for k in range(1, steps - 1):
+            g = steps + 1 + k
+            later.append(wall[3 + k : 4 + k] + half * wall[g : g + 1])
+        later.append(jnp.zeros_like(h))
+        later.append(wall[2 + steps :])
+        served[c] = jnp.concatenate(later, axis=0)
 
     def scatter(c):
         flow = flows_ref[pl.ds(c, 1), :]
@@ -427,101 +430,191 @@
         where = row_hot[c, :rows]
         added[...] += dot_nt(where, hot * hi) + dot_nt(where, hot * lo)
 
-    def beyond_z(step, f):
-        cur, new = step % 2, (step + 1) % 2
+    def beyond_z(step, cur, new, f):
         kappa = kappa_ref[f]
         beyond = halo_z[step, 0, f] * has_below
-        air[new, f, 1] += kappa * beyond + in_z_halo[...] * (beyond - air[cur, f, 1])
+        new[f, 1] += kappa * beyond + in_z_halo[...] * (beyond - cur[f, 1])
         beyond = halo_z[step, 1, f] * has_above
-        air[new, f, depth] += (speed[0, depth - 1] + kappa) * beyond
+        new[f, depth] += (speed[0, depth - 1] + kappa) * beyond
         beyond = halo_x[step, 0, f] * has_west
         fix_x[0, f] = kappa * beyond + in_x_halo[...] * (beyond - edge_x[step, 0, f])
         beyond = halo_x[step, 1, f] * has_east
         fix_x[1, f] = (out_x_last[...] + kappa) * beyond
 
-    def finish(step, chosen):
-        new = (step + 1) % 2
+    def finish(step, cur, new, chosen, walls_too=False):
         for f in chosen:
-            beyond_z(step, f)
-
-        def body(z, carry):
-            at = pl.ds(pl.multiple_of(z * breadth, breadth), breadth)
-            if 0 in chosen:
-                air[new, 0, z + 1] += added[at, :]
-            for f in chosen:
-                low = air[new, f, z + 1, 0:1, :] + fix_x[0, f, pl.ds(z, 1), :]
-                high = (
-                    air[new, f, z + 1, breadth - 1 : breadth, :] + fix_x[1, f, pl.ds(z, 1), :]
-                )
-                air[new, f, z + 1, 0:1, :] = low
-                air[new, f, z + 1, breadth - 1 : breadth, :] = high
-                if step + 1 < steps:
+            beyond_z(step, cur, new, f)
+
+        def body(k, carry):
+            for j in range(UNROLL):
+                z = k * UNROLL + j
+                if walls_too:
+                    at = pl.ds(pl.multiple_of(z * breadth, breadth), breadth)
+                    new[0, z + 1] += added[at, :]
+                for f in chosen:
+                    low = new[f, z + 1, 0:1, :] + fix_x[0, f, pl.ds(z, 1), :]
+                    high = (
+                        new[f, z + 1, breadth - 1 : breadth, :] + fix_x[1, f, pl.ds(z, 1), :]
+                    )
+                    new[f, z + 1, 0:1, :] = low
+                    new[f, z + 1, breadth - 1 : breadth, :] = high
                     edge_x[step + 1, 0, f, pl.ds(z, 1), :] = low
                     edge_x[step + 1, 1, f, pl.ds(z, 1), :] = high
             return carry
 
-        lax.fori_loop(0, depth, body, 0)
-
-    def wait_halos(step):
-        for copy in halo_copies(step, step % 2):
-            copy.wait()
-        if step == 0:
+        lax.fori_loop(0, depth // UNROLL, body, 0)
+
+    def store(f):
+        return pltpu.make_async_copy(
+            airs[steps % 2].at[f, pl.ds(1, depth)], air_out.at[f], store_sem.at[f]
+        )
+
+    rank_store = pltpu.make_async_copy(ranks_ref, ranks_out, store_sem.at[fields])
+    rank_store.start()
+    returned_store = pltpu.make_async_copy(returned, returned_out, store_sem.at[fields + 1])
+
+    beside = depth // chunks
+
+    def time_step(step, cur, new):
+        last = step == steps - 1
+
+        def body_gather(c, carry):
+            gather(step, c)
+            for k in range(beside):
+                stencil(cur, new, c * beside + k, range(1, fields))
+            return carry
+
+        lax.fori_loop(0, chunks, body_gather, 0)
+
+        @pl.when(last)
+        def _():
+            each(return_copy, lambda copy: copy.start())
+            returned[at_rows(me), :] = result[lax.div(me, per_chunk), :, at_lanes(me)]
+
+        @pl.when(step == 0)
+        def _():
             for copy in in_copies:
                 copy.wait()
             in_z_halo[...] = in_z_halo[...] * has_below
             in_x_halo[...] = in_x_halo[...] * has_west
 
-    def store(f):
-        return pltpu.make_async_copy(
-            air.at[steps % 2, f, pl.ds(1, depth)], air_out.at[f], store_sem.at[f]
-        )
-
-    for step in range(steps):
-        cur, new = step % 2, (step + 1) % 2
-        last = step == steps - 1
-        in_gather = 0 if step == 0 else depth // chunks if last else depth // chunks // 2
-        in_scatter = 0 if step == 0 else depth // chunks - in_gather
-
-        def body_gather(c, carry, step=step, cur=cur, new=new, count=in_gather):
-            gather(step, c)
-            for k in range(count):
-                stencil(cur, new, c * count + k)
+        for group in range(pairs):
+            chosen = [1 + group * paired + k for k in range(paired)]
+            for copy in halos_of(step, cur, group):
+                copy.wait()
+            finish(step, cur, new, chosen)
+
+            @pl.when(last)
+            def _():
+                for f in chosen:
+                    store(f).start()
+
+            @pl.when(jnp.logical_not(last))
+            def _():
+                for copy in halos_of(step + 1, new, group):
+                    copy.start()
+
+        added[...] = jnp.zeros_like(added)
+
+        def body_scatter(c, carry):
+            scatter(c)
+            for k in range(beside):
+                stencil(cur, new, c * beside + k, range(1))
             return carry
 
-        lax.fori_loop(0, chunks, body_gather, 0)
-        if last:
-            each(return_copy, lambda copy: copy.start())
-            returned[at_rows(me), :] = result[lax.div(me, per_chunk), :, at_lanes(me)]
-            wait_halos(step)
-            finish(step, range(1, fields))
-            for f in range(1, fields):
-                store(f).start()
-        added[...] = jnp.zeros_like(added)
-
-        def body_scatter(c, carry, cur=cur, new=new, count=in_scatter, first=in_gather * chunks):
-            scatter(c)
-            for k in range(count):
-                stencil(cur, new, first + c * count + k)
-            return carry
-
         lax.fori_loop(0, chunks, body_scatter, 0)
-        if last:
-            finish(step, range(1))
+        for copy in halos_of(step, cur, pairs):
+            copy.wait()
+        finish(step, cur, new, range(1), True)
+
+        @pl.when(last)
+        def _():
             store(0).start()
-        else:
-            wait_halos(step)
-            finish(step, range(fields))
-            for copy in halo_copies(step + 1, new):
+
+        @pl.when(jnp.logical_not(last))
+        def _():
+            for copy in halos_of(step + 1, new, pairs):
                 copy.start()
             split_field(new)
 
+    def two_steps(k, carry):
+        time_step(2 * k, air_even, air_odd)
+        time_step(2 * k + 1, air_odd, air_even)
+        return carry
+
+    lax.fori_loop(0, steps // 2, two_steps, 0)
     each(return_copy, lambda copy: copy.wait())
-    loads[8].wait()
-    placed = dot(jnp.concatenate(split(returned[...], 3), axis=0).astype(BF16), rank_hot[...])
+    returned_store.start()
+    for copy in [rank_store, returned_store] + [store(f) for f in range(fields)]:
+        copy.wait()
+
+
+def wall_kernel(
+    dims,
+    air_hbm,
+    returned_hbm,
+    ranks_hbm,
+    owner_hbm,
+    wall_hbm,
+    cond_hbm,
+    saved_hbm,
+    air_out,
+    wall_out,
+    grad_out,
+    air,
+    returned,
+    ranks_ref,
+    owner_ref,
+    wall_ref,
+    cond_ref,
+    saved_ref,
+    wall_res,
+    grad_res,
+    load_sem,
+    store_sem,
+):
+    steps, groups = dims
+    fields = air.shape[0]
+    cap = returned.shape[1]
+    walls = wall_ref.shape[1]
+    loads = [
+        pltpu.make_async_copy(src, dst, load_sem.at[k])
+        for k, (src, dst) in enumerate(
+            [(air_hbm.at[f], air.at[f]) for f in range(fields)]
+            + [
+                (ranks_hbm, ranks_ref),
+                (owner_hbm, owner_ref),
+                (returned_hbm, returned),
+                (wall_hbm, wall_ref),
+                (cond_hbm, cond_ref),
+                (saved_hbm, saved_ref),
+            ]
+        )
+    ]
+    for load in loads:
+        load.start()
+    stores = [
+        pltpu.make_async_copy(air.at[f], air_out.at[f], store_sem.at[f]) for f in range(fields)
+    ] + [
+        pltpu.make_async_copy(wall_res, wall_out, store_sem.at[fields]),
+        pltpu.make_async_copy(grad_res, grad_out, store_sem.at[fields + 1]),
+    ]
+    for f in range(fields):
+        loads[f].wait()
+        stores[f].start()
+    for load in loads[fields:]:
+        load.wait()
+    rank_hot = (
+        (lax.broadcasted_iota(I32, (cap, walls), 0) == ranks_ref[...]).astype(F32).astype(BF16)
+    )
+    owned = (lax.broadcasted_iota(I32, (groups, walls), 0) == owner_ref[...]).astype(F32)
+    placed = dot(jnp.concatenate(split(returned[...], 3), axis=0).astype(BF16), rank_hot)
+    n = groups * ROWS
     placed = placed[:n] + placed[n : 2 * n] + placed[2 * n :]
     flows = jnp.zeros((ROWS, walls), F32)
     for b in range(groups):
-        flows = flows + owned_ref[b : b + 1] * placed[b * ROWS : (b + 1) * ROWS]
+        flows = flows + owned[b : b + 1] * placed[b * ROWS : (b + 1) * ROWS]
+    surface = (lax.broadcasted_iota(I32, (ROWS, walls), 0) == 0).astype(F32)
     p = wall_ref[...]
     cond8 = jnp.concatenate([cond_ref[...], jnp.zeros((1, walls), F32)], axis=0)
     grad = jnp.zeros((ROWS, walls), F32)
@@ -531,13 +624,9 @@
         p = wall_back(p, cond8) - surface * flows[step : step + 1]
     wall_res[...] = p
     grad_res[...] = grad[: ROWS - 1]
-    stores = [
-        pltpu.make_async_copy(wall_res, wall_out, store_sem.at[fields]),
-        pltpu.make_async_copy(grad_res, grad_out, store_sem.at[fields + 1]),
-    ]
+    for copy in stores[fields:]:
+        copy.start()
     for copy in stores:
-        copy.start()
-    for copy in stores + [store(f) for f in range(fields)]:
         copy.wait()
 
 
@@ -561,6 +650,7 @@
     fields, depth, breadth, span = air_seed.shape
     rows = depth * breadth
     chunks = 2
+    pairs = 1
     chunk = groups * cap // chunks
     smem = pl.BlockSpec(memory_space=pltpu.SMEM)
     hbm = pl.BlockSpec(memory_space=pl.ANY)
@@ -571,11 +661,11 @@
     scratch = [
         pltpu.VMEM(wall_seed.shape, F32),
         pltpu.VMEM(conductivity.shape, F32),
-        pltpu.VMEM(wall_saved.shape, F32),
         pltpu.VMEM((1, walls), I32),
         pltpu.VMEM((1, walls), I32),
         pltpu.VMEM((1, walls), I32),
-        pltpu.VMEM((2, fields, depth + 2) + plane, F32),
+        pltpu.VMEM((fields, depth + 2) + plane, F32),
+        pltpu.VMEM((fields, depth + 2) + plane, F32),
         pltpu.VMEM((3,) + brick, F32),
         pltpu.VMEM((3,) + brick, I32),
         pltpu.VMEM((depth + 1,) + plane, F32),
@@ -588,7 +678,7 @@
         pltpu.VMEM(side, F32),
         pltpu.VMEM((steps, 2, fields) + plane, F32),
         pltpu.VMEM((steps, 2, fields) + side, F32),
-        pltpu.VMEM((steps, 2, fields) + side, F32),
+        pltpu.VMEM((steps + 1, 2, fields) + side, F32),
         pltpu.VMEM((2, fields) + side, F32),
         pltpu.VMEM((span, 2 * rows), BF16),
         pltpu.VMEM((chunks, 2 * rows, chunk), BF16),
@@ -597,32 +687,31 @@
         pltpu.VMEM((rows, span), F32),
         pltpu.VMEM((3 * groups * ROWS, walls), BF16),
         pltpu.VMEM((cap, walls), BF16),
-        pltpu.VMEM((groups, walls), F32),
+        pltpu.VMEM((1, walls), I32),
         pltpu.VMEM((groups * ROWS, cap), F32),
         pltpu.VMEM((chunks, ROWS, chunk), F32),
         pltpu.VMEM((chunks, ROWS, chunk), F32),
         pltpu.VMEM((groups * ROWS, cap), F32),
-        pltpu.VMEM(wall_seed.shape, F32),
-        pltpu.VMEM(conductivity.shape, F32),
-        dma((9,)),
+        dma((8,)),
         dma((fields + 2,)),
         dma((2,)),
         dma((2,)),
-        dma((steps, 4)),
-        dma((steps, 4)),
+        dma((steps, pairs + 1, 4)),
+        dma((steps, pairs + 1, 4)),
         dma((groups,)),
         dma((groups,)),
         dma((groups,)),
         dma((groups,)),
     ]
-    return pl.pallas_call(
+    owners = owner.reshape(1, walls)
+    air, returned, ranks = pl.pallas_call(
         functools.partial(kernel, (steps, groups, columns)),
         out_shape=(
             jax.ShapeDtypeStruct(air_seed.shape, F32),
-            jax.ShapeDtypeStruct(wall_seed.shape, F32),
-            jax.ShapeDtypeStruct(conductivity.shape, F32),
+            jax.ShapeDtypeStruct((groups * ROWS, cap), F32),
+            jax.ShapeDtypeStruct((1, walls), I32),
         ),
-        in_specs=[smem, smem] + [hbm] * 9,
+        in_specs=[smem, smem] + [hbm] * 8,
         out_specs=(hbm, hbm, hbm),
         scratch_shapes=scratch,
         compiler_params=pltpu.CompilerParams(
@@ -638,14 +727,42 @@
         heat_table,
         wall_seed,
         conductivity,
-        wall_saved,
         interface.reshape(1, walls),
-        owner.reshape(1, walls),
+        owners,
         material.reshape(1, walls),
         air_seed,
         speed,
         upwind,
     )
+    return pl.pallas_call(
+        functools.partial(wall_kernel, (steps, groups)),
+        out_shape=(
+            jax.ShapeDtypeStruct(air_seed.shape, F32),
+            jax.ShapeDtypeStruct(wall_seed.shape, F32),
+            jax.ShapeDtypeStruct(conductivity.shape, F32),
+        ),
+        in_specs=[hbm] * 7,
+        out_specs=(hbm, hbm, hbm),
+        scratch_shapes=[
+            pltpu.VMEM(air_seed.shape, F32),
+            pltpu.VMEM((groups * ROWS, cap), F32),
+            pltpu.VMEM((1, walls), I32),
+            pltpu.VMEM((1, walls), I32),
+            pltpu.VMEM(wall_seed.shape, F32),
+            pltpu.VMEM(conductivity.shape, F32),
+            pltpu.VMEM(wall_saved.shape, F32),
+            pltpu.VMEM(wall_seed.shape, F32),
+            pltpu.VMEM(conductivity.shape, F32),
+            dma((6 + fields,)),
+            dma((2 + fields,)),
+        ],
+        compiler_params=pltpu.CompilerParams(vmem_limit_bytes=VMEM_BYTES),
+        cost_estimate=pl.CostEstimate(
+            flops=2 * 3 * groups * ROWS * cap * walls,
+            bytes_accessed=48 * rows * span,
+            transcendentals=0,
+        ),
+    )(air, returned, ranks, owners, wall_seed, conductivity, wall_saved)
 
 
 def solution(mesh):

time: 60.5 us -> 56.1 us (0.927)
  local copies, waits for them, and re-layouts: 4.81 us -> 0 us
    unnamed x7 -> x0, local copies, waits for them, and re-layouts: 4.81 us -> none
    pallas_call x0 -> x1, Pallas kernels: none -> 2.96 us  [per_device(): pl.pallas_call(functools.partial(wall_kernel, (steps, groups)), out_shape...]
    pallas_call x1, Pallas kernels: 54.8 us -> 52.3 us  [per_device(): pl.pallas_call(functools.partial(kernel, (steps, groups, columns)), out_s...]
where the time goes in v2:
time: 56.1 us; the launch traced here: 55.9 us
  Pallas kernels  55.2 us (98%)
  between operations  0.64 us (1%)
    pallas_call x1, Pallas kernels, per_device(): pl.pallas_call(functools.partial(kernel, (steps, groups, columns)), out_s...  52.3 us
    pallas_call x1, Pallas kernels, per_device(): pl.pallas_call(functools.partial(wall_kernel, (steps, groups)), out_shape...  2.96 us

profile of v2, /device:TPU:1, one launch (start us, length us, event | category | flops | bytes accessed | tf_op | source)
XLA Modules:
  0.0 55.9 jit_solution(14687512253214684633)
XLA Ops:
  0.6 52.3 %shard_map.130 = (f32[5,16,32,256]{3,2,1,0:T(8,128)}, f32[128,256]{1,0:T(8,128)}, s32[1,1024]{1,0:T(1,128)}) custom-call(f32[5]{0:T(128)} %kappa_ref.1, f32[8]{0:T(128)} %table_ref.1, f32[8,1024]{1,0:T(8,128)} %wall_hbm.3, f32[7,1024]{1,0:T(8,128)} %cond_hbm.3, s32[1,1024]{1,0:T(1,128)} %bitcast.5, s32[1,1024]{1,0:T(1,128)} %bitcast.3, s32[1,1024]{1,0:T(1,128)} %bitcast.6, ...), custom_call_target="tpu_custom_call" | custom-call | flops 17179869184 | bytes 5242880 | tf_op jit(solution)/shard_map/pallas_call | solution.py:707
  52.9 3.0 %shard_map.131 = (f32[5,16,32,256]{3,2,1,0:T(8,128)}, f32[8,1024]{1,0:T(8,128)}, f32[7,1024]{1,0:T(8,128)}) custom-call(f32[5,16,32,256]{3,2,1,0:T(8,128)} %get-tuple-element.6.air_hbm, f32[128,256]{1,0:T(8,128)} %get-tuple-element.7.returned_hbm, s32[1,1024]{1,0:T(1,128)} %get-tuple-element.8.ranks_hbm, s32[1,1024]{1,0:T(1,128)} %bitcast.4, ...), custom_call_target="tpu_custom_call" | custom-call | flops 201326592 | bytes 6291456 | tf_op jit(solution)/shard_map/pallas_call | solution.py:737

commit v3 on v2

--- a/solution.py
+++ b/solution.py
@@ -389,6 +389,11 @@
                     total += (in_y[(z,) + at] + kappa) * south[h]
                     new[(f, z + 1) + at] = total
 
+    def stencil_first(z, carry):
+        stencil(air_even, air_odd, z, range(1, fields))
+        return carry
+
+    lax.fori_loop(0, depth, stencil_first, 0)
     each(parcel_copy, lambda copy: copy.wait())
 
     def one_hots(c, carry):
@@ -479,16 +484,35 @@
         last = step == steps - 1
 
         def body_gather(c, carry):
-            gather(step, c)
-            for k in range(beside):
-                stencil(cur, new, c * beside + k, range(1, fields))
+            @pl.when(step == 0)
+            def _():
+                gather(step, c)
+
+            @pl.when(step > 0)
+            def _():
+                gather(step, c)
+                for k in range(beside):
+                    stencil(cur, new, c * beside + k, range(1, fields))
+
+            @pl.when(last)
+            def _():
+                def send_back(k, carry):
+                    d = lax.rem(c * per_chunk + k - me + groups, groups)
+
+                    @pl.when(d > 0)
+                    def _():
+                        return_copy(d).start()
+
+                    return carry
+
+                lax.fori_loop(0, per_chunk, send_back, 0)
+
             return carry
 
         lax.fori_loop(0, chunks, body_gather, 0)
 
         @pl.when(last)
         def _():
-            each(return_copy, lambda copy: copy.start())
             returned[at_rows(me), :] = result[lax.div(me, per_chunk), :, at_lanes(me)]
 
         @pl.when(step == 0)

time: 56.1 us -> 54.6 us (0.973)
  Pallas kernels: 55.2 us -> 53.8 us
    pallas_call x1, Pallas kernels: 52.3 us -> 50.8 us  [per_device(): pl.pallas_call(functools.partial(kernel, (steps, groups, columns)), out_s...]
where the time goes in v3:
time: 54.6 us; the launch traced here: 54.4 us
  Pallas kernels  53.8 us (99%)
  between operations  0.64 us (1%)
    pallas_call x1, Pallas kernels, per_device(): pl.pallas_call(functools.partial(kernel, (steps, groups, columns)), out_s...  50.8 us
    pallas_call x1, Pallas kernels, per_device(): pl.pallas_call(functools.partial(wall_kernel, (steps, groups)), out_shape...  2.96 us

profile of v3, /device:TPU:1, one launch (start us, length us, event | category | flops | bytes accessed | tf_op | source)
XLA Modules:
  0.0 54.4 jit_solution(17595356119520493902)
XLA Ops:
  0.6 50.8 %shard_map.130 = (f32[5,16,32,256]{3,2,1,0:T(8,128)}, f32[128,256]{1,0:T(8,128)}, s32[1,1024]{1,0:T(1,128)}) custom-call(f32[5]{0:T(128)} %kappa_ref.1, f32[8]{0:T(128)} %table_ref.1, f32[8,1024]{1,0:T(8,128)} %wall_hbm.3, f32[7,1024]{1,0:T(8,128)} %cond_hbm.3, s32[1,1024]{1,0:T(1,128)} %bitcast.5, s32[1,1024]{1,0:T(1,128)} %bitcast.3, s32[1,1024]{1,0:T(1,128)} %bitcast.6, ...), custom_call_target="tpu_custom_call" | custom-call | flops 17179869184 | bytes 5242880 | tf_op jit(solution)/shard_map/pallas_call | solution.py:731
  51.5 3.0 %shard_map.131 = (f32[5,16,32,256]{3,2,1,0:T(8,128)}, f32[8,1024]{1,0:T(8,128)}, f32[7,1024]{1,0:T(8,128)}) custom-call(f32[5,16,32,256]{3,2,1,0:T(8,128)} %get-tuple-element.6.air_hbm, f32[128,256]{1,0:T(8,128)} %get-tuple-element.7.returned_hbm, s32[1,1024]{1,0:T(1,128)} %get-tuple-element.8.ranks_hbm, s32[1,1024]{1,0:T(1,128)} %bitcast.4, ...), custom_call_target="tpu_custom_call" | custom-call | flops 201326592 | bytes 6291456 | tf_op jit(solution)/shard_map/pallas_call | solution.py:761

commit v4 on v3

--- a/solution.py
+++ b/solution.py
@@ -390,7 +390,7 @@
                     new[(f, z + 1) + at] = total
 
     def stencil_first(z, carry):
-        stencil(air_even, air_odd, z, range(1, fields))
+        stencil(air_even, air_odd, z, range(fields))
         return carry
 
     lax.fori_loop(0, depth, stencil_first, 0)
@@ -482,19 +482,31 @@
 
     def time_step(step, cur, new):
         last = step == steps - 1
+        even = cur is air_even
+
+        def never(act):
+            return None
+
+        def always(act):
+            act()
+
+        when_first = pl.when(step == 0) if even else never
+        unless_first = pl.when(step > 0) if even else always
+        when_last = never if even else pl.when(last)
+        unless_last = always if even else pl.when(jnp.logical_not(last))
 
         def body_gather(c, carry):
-            @pl.when(step == 0)
+            @when_first
             def _():
                 gather(step, c)
 
-            @pl.when(step > 0)
+            @unless_first
             def _():
                 gather(step, c)
                 for k in range(beside):
-                    stencil(cur, new, c * beside + k, range(1, fields))
-
-            @pl.when(last)
+                    stencil(cur, new, c * beside + k, range(1, 1 + paired))
+
+            @when_last
             def _():
                 def send_back(k, carry):
                     d = lax.rem(c * per_chunk + k - me + groups, groups)
@@ -511,51 +523,61 @@
 
         lax.fori_loop(0, chunks, body_gather, 0)
 
-        @pl.when(last)
+        @when_last
         def _():
             returned[at_rows(me), :] = result[lax.div(me, per_chunk), :, at_lanes(me)]
 
-        @pl.when(step == 0)
+        @when_first
         def _():
             for copy in in_copies:
                 copy.wait()
             in_z_halo[...] = in_z_halo[...] * has_below
             in_x_halo[...] = in_x_halo[...] * has_west
 
-        for group in range(pairs):
+        def apply_halos(group):
             chosen = [1 + group * paired + k for k in range(paired)]
             for copy in halos_of(step, cur, group):
                 copy.wait()
             finish(step, cur, new, chosen)
 
-            @pl.when(last)
+            @when_last
             def _():
                 for f in chosen:
                     store(f).start()
 
-            @pl.when(jnp.logical_not(last))
+            @unless_last
             def _():
                 for copy in halos_of(step + 1, new, group):
                     copy.start()
 
+        apply_halos(0)
         added[...] = jnp.zeros_like(added)
 
         def body_scatter(c, carry):
-            scatter(c)
-            for k in range(beside):
-                stencil(cur, new, c * beside + k, range(1))
+            @when_first
+            def _():
+                scatter(c)
+
+            @unless_first
+            def _():
+                scatter(c)
+                for k in range(beside):
+                    stencil(cur, new, c * beside + k, [0, *range(1 + paired, fields)])
+
             return carry
 
         lax.fori_loop(0, chunks, body_scatter, 0)
+        for group in range(1, pairs):
+            apply_halos(group)
         for copy in halos_of(step, cur, pairs):
             copy.wait()
         finish(step, cur, new, range(1), True)
 
-        @pl.when(last)
+        @when_last
         def _():
             store(0).start()
 
-        @pl.when(jnp.logical_not(last))
+        @unless_last
         def _():
             for copy in halos_of(step + 1, new, pairs):
                 copy.start()
@@ -674,7 +696,7 @@
     fields, depth, breadth, span = air_seed.shape
     rows = depth * breadth
     chunks = 2
-    pairs = 1
+    pairs = 2
     chunk = groups * cap // chunks
     smem = pl.BlockSpec(memory_space=pltpu.SMEM)
     hbm = pl.BlockSpec(memory_space=pl.ANY)

time: 54.6 us -> 53.7 us (0.984)
  Pallas kernels: 53.8 us -> 52.9 us
    pallas_call x1, Pallas kernels: 50.8 us -> 50 us  [per_device(): pl.pallas_call(functools.partial(kernel, (steps, groups, columns)), out_s...]
where the time goes in v4:
time: 53.7 us; the launch traced here: 53.6 us
  Pallas kernels  52.9 us (99%)
  between operations  0.64 us (1%)
    pallas_call x1, Pallas kernels, per_device(): pl.pallas_call(functools.partial(kernel, (steps, groups, columns)), out_s...  50 us
    pallas_call x1, Pallas kernels, per_device(): pl.pallas_call(functools.partial(wall_kernel, (steps, groups)), out_shape...  2.96 us

profile of v4, /device:TPU:1, one launch (start us, length us, event | category | flops | bytes accessed | tf_op | source)
XLA Modules:
  0.0 53.6 jit_solution(17648394789567627914)
XLA Ops:
  0.6 50.0 %shard_map.130 = (f32[5,16,32,256]{3,2,1,0:T(8,128)}, f32[128,256]{1,0:T(8,128)}, s32[1,1024]{1,0:T(1,128)}) custom-call(f32[5]{0:T(128)} %kappa_ref.1, f32[8]{0:T(128)} %table_ref.1, f32[8,1024]{1,0:T(8,128)} %wall_hbm.3, f32[7,1024]{1,0:T(8,128)} %cond_hbm.3, s32[1,1024]{1,0:T(1,128)} %bitcast.5, s32[1,1024]{1,0:T(1,128)} %bitcast.3, s32[1,1024]{1,0:T(1,128)} %bitcast.6, ...), custom_call_target="tpu_custom_call" | custom-call | flops 17179869184 | bytes 5242880 | tf_op jit(solution)/shard_map/pallas_call | solution.py:753
  50.6 3.0 %shard_map.131 = (f32[5,16,32,256]{3,2,1,0:T(8,128)}, f32[8,1024]{1,0:T(8,128)}, f32[7,1024]{1,0:T(8,128)}) custom-call(f32[5,16,32,256]{3,2,1,0:T(8,128)} %get-tuple-element.6.air_hbm, f32[128,256]{1,0:T(8,128)} %get-tuple-element.7.returned_hbm, s32[1,1024]{1,0:T(1,128)} %get-tuple-element.8.ranks_hbm, s32[1,1024]{1,0:T(1,128)} %bitcast.4, ...), custom_call_target="tpu_custom_call" | custom-call | flops 201326592 | bytes 6291456 | tf_op jit(solution)/shard_map/pallas_call | solution.py:783
